TPU v7x, 128 devices: a whole 4x4x4 slice. The times are simulated.
128 devices in a mesh: row: 8 (over x_lo, z), col: 16 (over x_hi, y, core).
Axes of the slice: x: 4 (x_hi: 2, x_lo: 2; x = x_hi * 2 + x_lo), y: 4, z: 4, core: 2. Of those that a mesh axis runs over, the one named last changes fastest.
Arguments:
- inverse_block: float32 [12288, 12288], P('row', 'col'), may hold values from -0.14433757 to 0.14433757, as said below
- grid_position: int32 [12288], replicated, may hold values from 0 to 12287, each once
- panel_a: float32 [512, 12288], P('row', 'col'), may hold values from -1.5 to 1.5
- pivot_inverse_a: float32 [512, 512], replicated, may hold values from -6 to 6
- chosen_rows: int32 [8192], replicated, may hold values from 0 to 12287, as said below
- top_panel_b: float32 [512, 512], replicated, may hold values from -1.5 to 1.5
- panel_b: float32 [512, 8192], P('row', 'col'), may hold values from -1.5 to 1.5
- pivot_inverse_b: float32 [512, 512], replicated, may hold values from -6 to 6
Outputs:
- inverse_panel_a: float32 [12288, 512], P(('row', 'col'))
- diagonal_a: float32 [512, 512], replicated
- inverse_panel_b: float32 [12288, 512], P(('row', 'col'))
- inverse_top_b: float32 [512, 512], replicated
- diagonal_b: float32 [512, 512], replicated
Inputs may be any that keep to these rules, and one draw needn't show every extreme that they name: `grid_position`: each of 0 to 12287 appears once. `chosen_rows`: 8192 distinct values. `inverse_block`: symmetric: entry (i, j) equals entry (j, i) in grid storage order.
All inputs are finite; a program needn't handle non-finite values.
Results may differ from a plain program's by a relative error of at most 0.00008.
Values sent between devices are 32-bit elements; how exact they have to be, the bound alone decides.
A program may use at most 128 MiB of HBM per device.

v0:
```python
import jax
import jax.numpy as jnp
from jax import lax
from jax.sharding import PartitionSpec as P


def pick_columns(wide, index, limit):
    valid = (index < limit).astype(jnp.float32)
    taken = jnp.take(wide, jnp.minimum(index, limit - 1), axis=1)
    return taken * valid[None, :]


def select_columns(wide, source, start, length, limit):
    index = lax.dynamic_slice_in_dim(source, start, length, 0)
    return pick_columns(wide, index, limit)


def project(block, panel_t):
    return lax.dot_general(
        block,
        panel_t,
        (((1,), (1,)), ((), ())),
        precision=lax.Precision.HIGHEST,
        preferred_element_type=jnp.float32,
    )


def body(
    inverse_block,
    grid_position,
    panel_a,
    pivot_inverse_a,
    chosen_rows,
    top_panel_b,
    panel_b,
    pivot_inverse_b,
):
    exact = lax.Precision.HIGHEST
    rows_here = inverse_block.shape[0]
    cols_here = inverse_block.shape[1]
    order = grid_position.shape[0]
    count = chosen_rows.shape[0]
    row_count = lax.axis_size("row")
    own_rows = rows_here // lax.axis_size("col")
    col_start = lax.axis_index("col") * cols_here
    own_start = lax.axis_index("row") * rows_here + lax.axis_index("col") * own_rows
    group_starts = (
        jnp.arange(row_count, dtype=jnp.int32) * rows_here + lax.axis_index("col") * own_rows
    )
    group_index = (group_starts[:, None] + jnp.arange(own_rows, dtype=jnp.int32)[None, :]).reshape(
        -1
    )
    local_offset = lax.axis_index("row") * own_rows
    source_a = (
        jnp.zeros((order,), jnp.int32).at[grid_position].set(jnp.arange(order, dtype=jnp.int32))
    )
    source_b = (
        jnp.full((order,), count, jnp.int32)
        .at[grid_position[chosen_rows]]
        .set(jnp.arange(count, dtype=jnp.int32))
    )
    group_a = source_a[group_index]
    group_b = source_b[group_index]
    valid_own = (lax.dynamic_slice_in_dim(source_b, own_start, own_rows, 0) < count).astype(
        jnp.float32
    )
    wide_a = lax.all_gather(panel_a, "col", axis=1, tiled=True)
    cols_a, group_own_a = (
        lax.all_gather(
            select_columns(wide_a, source_a, col_start, cols_here, order), "row", axis=0, tiled=True
        ),
        lax.all_gather(pick_columns(wide_a, group_a, order), "row", axis=0, tiled=True),
    )
    product_a = lax.psum_scatter(
        project(inverse_block, cols_a), "col", scatter_dimension=0, tiled=True
    )
    wide_b = lax.all_gather(panel_b, "col", axis=1, tiled=True)
    cols_b, group_own_b = (
        lax.all_gather(
            select_columns(wide_b, source_b, col_start, cols_here, count), "row", axis=0, tiled=True
        ),
        lax.all_gather(pick_columns(wide_b, group_b, count), "row", axis=0, tiled=True),
    )
    product_b = lax.psum_scatter(
        project(inverse_block, cols_b), "col", scatter_dimension=0, tiled=True
    )
    own_a = lax.dynamic_slice_in_dim(group_own_a, local_offset, own_rows, 1)
    own_b = lax.dynamic_slice_in_dim(group_own_b, local_offset, own_rows, 1)
    inverse_panel_a = -product_a
    diag_part = jnp.dot(own_a, inverse_panel_a, precision=exact, preferred_element_type=jnp.float32)
    cross_part = lax.dot_general(
        inverse_panel_a,
        own_b,
        (((0,), (1,)), ((), ())),
        precision=exact,
        preferred_element_type=jnp.float32,
    )
    diag_total, cross = lax.psum((diag_part, cross_part), ("row", "col"))
    diagonal_a = pivot_inverse_a - diag_total
    inverse_top_b = -(
        jnp.dot(diagonal_a, top_panel_b, precision=exact, preferred_element_type=jnp.float32)
        + cross
    )
    bottom = product_b + jnp.dot(
        inverse_panel_a, top_panel_b, precision=exact, preferred_element_type=jnp.float32
    )
    inverse_panel_b = -bottom * valid_own[:, None]
    last_part = jnp.dot(own_b, inverse_panel_b, precision=exact, preferred_element_type=jnp.float32)
    last_total = lax.psum(last_part, ("row", "col"))
    diagonal_b = (
        pivot_inverse_b
        - jnp.dot(top_panel_b.T, inverse_top_b, precision=exact, preferred_element_type=jnp.float32)
        - last_total
    )
    return (inverse_panel_a, diagonal_a, inverse_panel_b, inverse_top_b, diagonal_b)


def solution(mesh):
    in_specs = (P("row", "col"), P(), P("row", "col"), P(), P(), P(), P("row", "col"), P())
    out_specs = (P(("row", "col"), None), P(), P(("row", "col"), None), P(), P())
    return jax.shard_map(body, mesh=mesh, in_specs=in_specs, out_specs=out_specs, check_vma=False)
```

profile of v0, /device:TPU:1, one launch (start us, length us, event | category | flops | bytes accessed | tf_op | source)
XLA Modules:
  0.0 630.5 jit_solution(11764547674448368654)
XLA Ops:
  7.2 1.9 copy.40
  9.2 1.7 copy.43
  11.9 45.4 %scatter_custom_fusion = s32[12288]{0:T(1024)S(1)} fusion(s32[12288]{0:T(1024)S(1)} %compare_select_fusion.1, s32[12288]{0:T(1024)S(1)} %iota.15, s32[]{:T(128)} %constant.4.clone.1), kind=kCustom, calls=%fused_computation.35 | custom fusion | bytes 49156 | tf_op jit(solution)/shard_map/scatter | solution.py:55
  57.4 21.3 %all-gather.7.cloned.1.call-done = f32[64,12288]{0,1:T(8,128)} async-done(((f32[64,768]{0,1:T(8,128)}), f32[64,12288]{0,1:T(8,128)}) %all-gather.7.cloned.1.call-update) | async-done | bytes 3145744 | tf_op jit(solution)/shard_map/all_gather | solution.py:67
  78.7 4.3 gather_fusion.3
  84.1 45.5 %gather_fusion.1 = s32[8192]{0:T(1024)S(1)} fusion(s32[12288]{0:T(1024)S(1)} %copy-done.1, s32[8192]{0:T(1024)S(1)} %fusion.11), kind=kCustom, calls=%fused_computation.5 | custom fusion | bytes 98304 | tf_op jit(solution)/shard_map/gather | solution.py:59
  129.7 30.5 %scatter_custom_fusion.1 = s32[12288]{0:T(1024)S(1)} fusion(s32[8192]{0:T(1024)S(1)} %bitcast.35, s32[8192]{0:T(1024)S(1)} %iota.17, s32[]{:T(128)} %constant.36.clone.1), kind=kCustom, calls=%fused_computation.33 | custom fusion | bytes 49156 | tf_op jit(solution)/shard_map/scatter | solution.py:60
  160.3 3.8 gather_fusion.5
  165.0 4.1 all-gather.9.cloned.1.call-done
  169.1 11.3 %convolution_bitcast_fusion.1 = f32[1536,512]{0,1:T(8,128)} fusion(f32[512,768]{1,0:T(8,128)} %all-gather.9.cloned.1.call-done, f32[1536,768]{1,0:T(8,128)} %param.12), kind=kOutput, calls=%fused_computation.10 | convolution fusion | flops 7247757312 | bytes 9437184 | tf_op jit(solution)/shard_map/dot_general | solution.py:19
  180.3 3.7 copy.52
  184.3 4.5 gather_fusion
  188.8 4.4 gather_fusion.4
  194.1 4.5 gather_fusion.2
  198.6 3.8 gather_fusion.6
  203.5 7.6 %all-gather.15.cloned.1.call-done = f32[512,768]{1,0:T(8,128)} async-done(((f32[64,768]{1,0:T(8,128)}), f32[512,768]{1,0:T(8,128)}) %all-gather.15.cloned.1.call-update) | async-done | bytes 1572880 | tf_op jit(solution)/shard_map/all_gather | solution.py:79
  211.0 11.3 %convolution_bitcast_fusion = f32[1536,512]{0,1:T(8,128)} fusion(f32[512,768]{1,0:T(8,128)} %all-gather.15.cloned.1.call-done, f32[1536,768]{1,0:T(8,128)} %param.12), kind=kOutput, calls=%fused_computation.9 | convolution fusion | flops 7247757312 | bytes 9437184 | tf_op jit(solution)/shard_map/dot_general | solution.py:19
  222.4 3.5 copy.54
  226.0 68.4 %reduce-scatter.7.cloned.1.call-done = f32[96,512]{1,0:T(8,128)} async-done(((f32[1536,512]{1,0:T(8,128)}), f32[96,512]{1,0:T(8,128)}) %reduce-scatter.7.cloned.1.call-update) | async-done | bytes 196624
  295.5 35.6 %all-gather.11.cloned.1.call-done = f32[512,768]{1,0:T(8,128)} async-done(((f32[64,768]{1,0:T(8,128)}), f32[512,768]{1,0:T(8,128)}) %all-gather.11.cloned.1.call-update) | async-done | bytes 1572880 | tf_op jit(solution)/shard_map/all_gather | solution.py:72
  331.1 3.0 fusion.5
  334.1 39.1 %all-gather.17.cloned.1.call-done = f32[512,768]{1,0:T(8,128)} async-done(((f32[64,768]{1,0:T(8,128)}), f32[512,768]{1,0:T(8,128)}) %all-gather.17.cloned.1.call-update) | async-done | bytes 1572880 | tf_op jit(solution)/shard_map/all_gather | solution.py:82
  373.2 3.1 fusion.9
  376.3 80.5 %reduce-scatter.9.cloned.1.call-done = f32[96,512]{1,0:T(8,128)} async-done(((f32[1536,512]{1,0:T(8,128)}), f32[96,512]{1,0:T(8,128)}) %reduce-scatter.9.cloned.1.call-update) | async-done | bytes 196624 | tf_op jit(solution)/shard_map/reduce_scatter | solution.py:84
  456.8 1.7 fusion.4
  459.2 3.1 fusion.7
  462.3 1.6 copy.47
  464.7 1.8 copy.49
  466.5 149.7 %all-reduce.3.cloned.1.call-done = (f32[512,512]{1,0:T(8,128)}, f32[512,512]{1,0:T(8,128)}, f32[512,512]{0,1:T(8,128)}) async-done(((f32[512,512]{1,0:T(8,128)}, f32[512,512]{1,0:T(8,128)}, f32[512,512]{0,1:T(8,128)}), (f32[512,512]{1,0:T(8,128)}, f32[512,512]{1,0:T(8,128)}, f32[512,512]{0,1:T(8,128)})) %all-reduce.3.cloned.1.call-update) | async-done | bytes 3145744 | tf_op jit(solution)/shard_map/psum | solution.py:98
  616.2 1.6 sub.9
  617.8 1.9 fusion.2
  620.6 2.0 fusion.1
  (69 shorter events, 10.2 us)
Async XLA Ops:
  7.2 449.7 %copy-start = (f32[512,512]{1,0:T(8,128)S(1)}, f32[512,512]{1,0:T(8,128)}, u32[]{:S(2)}) copy-start(f32[512,512]{1,0:T(8,128)} %param.17) | copy-start | bytes 3145732
  7.2 76.9 %copy-start.1 = (s32[12288]{0:T(1024)S(1)}, s32[12288]{0:T(1024)}, u32[]{:S(2)}) copy-start(s32[12288]{0:T(1024)} %param.13) | copy-start | bytes 147460
  7.2 76.8 %copy-start.8 = (s32[8192]{0:T(1024)S(1)}, s32[8192]{0:T(1024)}, u32[]{:S(2)}) copy-start(s32[8192]{0:T(1024)} %param.16) | copy-start | bytes 98308
  7.2 71.5 %all-gather.7.cloned.1.call-start = ((), (), s32[]{:S(2)}) async-start(), calls=%async_computation.2 | async-start | bytes 6684672 | tf_op jit(solution)/shard_map/all_gather | solution.py:67
  9.2 151.1 %all-gather.13.cloned.1.call-start = ((), (), s32[]{:S(2)}) async-start(), calls=%async_computation.5 | async-start | bytes 4456448 | tf_op jit(solution)/shard_map/all_gather | solution.py:77
  11.0 158.0 %all-gather.9.cloned.1.call-start = ((), (), s32[]{:S(2)}) async-start(), calls=%async_computation.3 | async-start | bytes 1769472 | tf_op jit(solution)/shard_map/all_gather | solution.py:69
  84.0 127.1 %all-gather.15.cloned.1.call-start = ((), (), s32[]{:S(2)}) async-start(), calls=%async_computation.6 | async-start | bytes 1769472 | tf_op jit(solution)/shard_map/all_gather | solution.py:79
  164.9 129.5 %reduce-scatter.7.cloned.1.call-start = ((), (), s32[]{:S(2)}) async-start(), calls=%async_computation.8 | async-start | bytes 3342336
  184.0 147.1 %all-gather.11.cloned.1.call-start = ((), (), s32[]{:S(2)}) async-start(), calls=%async_computation.4 | async-start | bytes 1769472 | tf_op jit(solution)/shard_map/all_gather | solution.py:72
  194.0 179.2 %all-gather.17.cloned.1.call-start = ((), (), s32[]{:S(2)}) async-start(), calls=%async_computation.7 | async-start | bytes 1769472 | tf_op jit(solution)/shard_map/all_gather | solution.py:82
  203.3 253.6 %reduce-scatter.9.cloned.1.call-start = ((), (), s32[]{:S(2)}) async-start(), calls=%async_computation.9 | async-start | bytes 3342336 | tf_op jit(solution)/shard_map/reduce_scatter | solution.py:84
  225.9 390.3 %all-reduce.3.cloned.1.call-start = ((), (), s32[]{:S(2)}) async-start(), calls=%async_computation.10 | async-start | bytes 6291456 | tf_op jit(solution)/shard_map/psum | solution.py:98
  458.5 0.7 copy-start.7
  462.3 153.9 %copy-start.4 = (f32[512,512]{1,0:T(8,128)S(1)}, f32[512,512]{1,0:T(8,128)}, u32[]{:S(2)}) copy-start(f32[512,512]{1,0:T(8,128)} %param.15) | copy-start | bytes 3145732
  616.2 1.6 copy-start.6
  616.2 4.5 copy-start.5
  617.7 1.9 copy-start.2
  619.6 1.0 copy-start.3
Sparse Core Ops, SparseCore 0:
  11.1 67.6 all-gather.6
  81.8 53.0 all-gather.12
  137.1 31.9 all-gather.8
  171.1 39.8 all-gather.14
  214.9 79.4 reduce-scatter.6
  296.5 34.5 all-gather.10
  333.3 39.8 all-gather.16
  377.3 79.5 reduce-scatter.8
  462.5 153.5 all-reduce.2
where the time goes:
time: 631 us; the launch traced here: 630 us
  waiting for transfers between devices  406 us (64%)
  local copies, waits for them, and re-layouts  166 us (26%)
  matrix products  37.4 us (6%)
  between operations  14.2 us (2%)
  other arithmetic  6.35 us (1%)
    psum x1, waiting for transfers between devices, body(): diag_total, cross = lax.psum((diag_part, cross_part), ('row', 'col'))  150 us
    reduce_scatter x1, waiting for transfers between devices, body(): lax.psum_scatter(project(inverse_block, cols_b), 'col', scatter_dimension...  80.5 us
    unnamed x10, waiting for transfers between devices  68.6 us
    gather x1, local copies, waits for them, and re-layouts, body(): grid_position[chosen_rows]  45.5 us
    scatter x1, local copies, waits for them, and re-layouts, body(): jnp.zeros((order,), jnp.int32).at[grid_position]  45.4 us
    all_gather x1, waiting for transfers between devices, body(): lax.all_gather(pick_columns(wide_b, group_b, count), 'row', axis=0, tiled...  39.1 us
    all_gather x1, waiting for transfers between devices, body(): lax.all_gather(pick_columns(wide_a, group_a, order), 'row', axis=0, tiled...  35.6 us
    scatter x1, local copies, waits for them, and re-layouts, body(): source_b = jnp.full((order,), count, jnp.int32).at[grid_position[chosen_r...  30.5 us
  transfers between devices with their start and end apart: 9, of which 8 were waited for; matrix products, arithmetic and copies ran while one was open for 31% of the time, Pallas kernels for 0%

commit v1 on v0

--- a/solution.py
+++ b/solution.py
@@ -95,7 +95,7 @@
         precision=exact,
         preferred_element_type=jnp.float32,
     )
-    diag_total, cross = lax.psum((diag_part, cross_part), ("row", "col"))
+    diag_total, cross = lax.psum(lax.psum((diag_part, cross_part), "col"), "row")
     diagonal_a = pivot_inverse_a - diag_total
     inverse_top_b = -(
         jnp.dot(diagonal_a, top_panel_b, precision=exact, preferred_element_type=jnp.float32)

time: 631 us -> 858 us (1.36)
  waiting for transfers between devices: 406 us -> 632 us
    psum x1 -> x3, waiting for transfers between devices: 150 us -> 361 us  [the longest x1 151 us: body(): last_total = lax.psum(last_part, ('row', 'col'))]
    unnamed x10 -> x12, waiting for transfers between devices: 68.6 us -> 24.3 us
    all_gather x1, waiting for transfers between devices: 7.55 us -> 38.9 us  [body(): lax.all_gather(select_columns(wide_b, source_b, col_start, cols_here, cou...]
    all_gather x1, waiting for transfers between devices: 4.08 us -> 31.1 us  [body(): lax.all_gather(select_columns(wide_a, source_a, col_start, cols_here, ord...]
    unnamed x26 -> x24, local copies, waits for them, and re-layouts: 18.2 us -> 16.6 us
  transfers between devices with their start and end apart: 9 -> 11, of which waited for: 8 -> 10; matrix products, arithmetic and copies ran while one was open for 31% -> 23% of each run, Pallas kernels for 0% -> 0%
where the time goes in v1:
time: 858 us
  waiting for transfers between devices  632 us (74%)
  local copies, waits for them, and re-layouts  164 us (19%)
  matrix products  40 us (5%)
  between operations  14.2 us (2%)
    psum x1, waiting for transfers between devices, body(): last_total = lax.psum(last_part, ('row', 'col'))  151 us
    psum x1, waiting for transfers between devices, body(): lax.psum((diag_part, cross_part), 'col')  137 us
    reduce_scatter x1, waiting for transfers between devices, body(): lax.psum_scatter(project(inverse_block, cols_b), 'col', scatter_dimension...  79.1 us
    psum x1, waiting for transfers between devices, body(): lax.psum(lax.psum((diag_part, cross_part), 'col'), 'row')  72.3 us
    gather x1, local copies, waits for them, and re-layouts, body(): grid_position[chosen_rows]  45.5 us
    scatter x1, local copies, waits for them, and re-layouts, body(): jnp.zeros((order,), jnp.int32).at[grid_position]  45.4 us
    all_gather x1, waiting for transfers between devices, body(): lax.all_gather(select_columns(wide_b, source_b, col_start, cols_here, cou...  38.9 us
    all_gather x1, waiting for transfers between devices, body(): lax.all_gather(pick_columns(wide_b, group_b, count), 'row', axis=0, tiled...  38.9 us
  transfers between devices with their start and end apart: 11, of which 10 were waited for; matrix products, arithmetic and copies ran while one was open for 23% of the time, Pallas kernels for 0%

profile of v1, /device:TPU:1, one launch (start us, length us, event | category | flops | bytes accessed | tf_op | source)
XLA Modules:
  0.0 857.6 jit_solution(6523447706915437993)
XLA Ops:
  7.2 1.9 copy.40
  10.1 45.4 %scatter_custom_fusion = s32[12288]{0:T(1024)S(1)} fusion(s32[12288]{0:T(1024)S(1)} %compare_select_fusion.1, s32[12288]{0:T(1024)S(1)} %iota.15, s32[]{:T(128)} %constant.4.clone.1), kind=kCustom, calls=%fused_computation.35 | custom fusion | bytes 49156 | tf_op jit(solution)/shard_map/scatter | solution.py:55
  55.6 23.1 %all-gather.7.cloned.1.call-done = f32[64,12288]{0,1:T(8,128)} async-done(((f32[64,768]{0,1:T(8,128)}), f32[64,12288]{0,1:T(8,128)}) %all-gather.7.cloned.1.call-update) | async-done | bytes 3145744 | tf_op jit(solution)/shard_map/all_gather | solution.py:67
  78.7 4.3 gather_fusion.3
  84.9 31.1 %all-gather.9.cloned.1.call-done = f32[512,768]{1,0:T(8,128)} async-done(((f32[64,768]{1,0:T(8,128)}), f32[512,768]{1,0:T(8,128)}) %all-gather.9.cloned.1.call-update) | async-done | bytes 1572880 | tf_op jit(solution)/shard_map/all_gather | solution.py:69
  116.0 11.3 %convolution_bitcast_fusion.1 = f32[1536,512]{0,1:T(8,128)} fusion(f32[512,768]{1,0:T(8,128)} %all-gather.9.cloned.1.call-done, f32[1536,768]{1,0:T(8,128)} %param.12), kind=kOutput, calls=%fused_computation.10 | convolution fusion | flops 7247757312 | bytes 9437184 | tf_op jit(solution)/shard_map/dot_general | solution.py:19
  127.4 3.7 copy.52
  131.4 4.5 gather_fusion
  135.9 4.4 gather_fusion.4
  141.2 45.5 %gather_fusion.1 = s32[8192]{0:T(1024)S(1)} fusion(s32[12288]{0:T(1024)S(1)} %copy-done.1, s32[8192]{0:T(1024)S(1)} %fusion.11), kind=kCustom, calls=%fused_computation.5 | custom fusion | bytes 98304 | tf_op jit(solution)/shard_map/gather | solution.py:59
  186.8 30.5 %scatter_custom_fusion.1 = s32[12288]{0:T(1024)S(1)} fusion(s32[8192]{0:T(1024)S(1)} %bitcast.35, s32[8192]{0:T(1024)S(1)} %iota.17, s32[]{:T(128)} %constant.36.clone.1), kind=kCustom, calls=%fused_computation.33 | custom fusion | bytes 49156 | tf_op jit(solution)/shard_map/scatter | solution.py:60
  217.3 4.5 gather_fusion.2
  221.8 3.8 gather_fusion.6
  226.6 3.8 gather_fusion.5
  231.5 24.1 %reduce-scatter.7.cloned.1.call-done = f32[96,512]{1,0:T(8,128)} async-done(((f32[1536,512]{1,0:T(8,128)}), f32[96,512]{1,0:T(8,128)}) %reduce-scatter.7.cloned.1.call-update) | async-done | bytes 196624
  256.7 35.6 %all-gather.11.cloned.1.call-done = f32[512,768]{1,0:T(8,128)} async-done(((f32[64,768]{1,0:T(8,128)}), f32[512,768]{1,0:T(8,128)}) %all-gather.11.cloned.1.call-update) | async-done | bytes 1572880 | tf_op jit(solution)/shard_map/all_gather | solution.py:72
  292.2 3.0 fusion.5
  295.3 38.9 %all-gather.17.cloned.1.call-done = f32[512,768]{1,0:T(8,128)} async-done(((f32[64,768]{1,0:T(8,128)}), f32[512,768]{1,0:T(8,128)}) %all-gather.17.cloned.1.call-update) | async-done | bytes 1572880 | tf_op jit(solution)/shard_map/all_gather | solution.py:82
  334.2 3.1 fusion.9
  337.4 38.9 %all-gather.15.cloned.1.call-done = f32[512,768]{1,0:T(8,128)} async-done(((f32[64,768]{1,0:T(8,128)}), f32[512,768]{1,0:T(8,128)}) %all-gather.15.cloned.1.call-update) | async-done | bytes 1572880 | tf_op jit(solution)/shard_map/all_gather | solution.py:79
  376.3 11.4 %convolution_bitcast_fusion = f32[1536,512]{0,1:T(8,128)} fusion(f32[512,768]{1,0:T(8,128)} %all-gather.15.cloned.1.call-done, f32[1536,768]{1,0:T(8,128)} %param.12), kind=kOutput, calls=%fused_computation.9 | convolution fusion | flops 7247757312 | bytes 9437184 | tf_op jit(solution)/shard_map/dot_general | solution.py:19
  387.7 3.5 copy.54
  391.3 137.5 %all-reduce.8.cloned.1.call-done = (f32[512,512]{1,0:T(8,128)}, f32[512,512]{1,0:T(8,128)}) async-done(((f32[512,512]{1,0:T(8,128)}, f32[512,512]{1,0:T(8,128)}), (f32[512,512]{1,0:T(8,128)}, f32[512,512]{1,0:T(8,128)})) %all-reduce.8.cloned.1.call-update) | async-done | bytes 2097168 | tf_op jit(solution)/shard_map/psum | solution.py:98
  529.2 79.1 %reduce-scatter.9.cloned.1.call-done = f32[96,512]{1,0:T(8,128)} async-done(((f32[1536,512]{1,0:T(8,128)}), f32[96,512]{1,0:T(8,128)}) %reduce-scatter.9.cloned.1.call-update) | async-done | bytes 196624 | tf_op jit(solution)/shard_map/reduce_scatter | solution.py:84
  608.3 1.7 fusion.4
  610.0 3.2 fusion.7
  613.2 1.6 copy.47
  615.5 1.8 copy.49
  617.3 72.3 %all-reduce.10.cloned.1.call-done = (f32[512,512]{1,0:T(8,128)}, f32[512,512]{1,0:T(8,128)}) async-done(((f32[512,512]{1,0:T(8,128)}, f32[512,512]{1,0:T(8,128)}), (f32[512,512]{1,0:T(8,128)}, f32[512,512]{1,0:T(8,128)})) %all-reduce.10.cloned.1.call-update) | async-done | bytes 2097168 | tf_op jit(solution)/shard_map/psum | solution.py:98
  692.0 2.8 fusion.2
  694.9 151.5 %all-reduce.6.cloned.1.call-done = f32[512,512]{0,1:T(8,128)} async-done(((f32[512,512]{0,1:T(8,128)}), f32[512,512]{0,1:T(8,128)}) %all-reduce.6.cloned.1.call-update) | async-done | bytes 1048592 | tf_op jit(solution)/shard_map/psum | solution.py:109
  846.3 3.4 fusion.1
  (73 shorter events, 12.2 us)
Async XLA Ops:
  7.2 601.1 %copy-start = (f32[512,512]{1,0:T(8,128)S(1)}, f32[512,512]{1,0:T(8,128)}, u32[]{:S(2)}) copy-start(f32[512,512]{1,0:T(8,128)} %param.17) | copy-start | bytes 3145732
  7.2 76.8 %copy-start.6 = (f32[64,512]{1,0:T(8,128)S(1)}, f32[64,512]{1,0:T(8,128)}, u32[]{:S(2)}) copy-start(f32[64,512]{1,0:T(8,128)} %param.18) | copy-start | bytes 393220
  7.2 71.5 %all-gather.7.cloned.1.call-start = ((), (), s32[]{:S(2)}) async-start(), calls=%async_computation.2 | async-start | bytes 6684672 | tf_op jit(solution)/shard_map/all_gather | solution.py:67
  9.2 106.9 %all-gather.9.cloned.1.call-start = ((), (), s32[]{:S(2)}) async-start(), calls=%async_computation.3 | async-start | bytes 1769472 | tf_op jit(solution)/shard_map/all_gather | solution.py:69
  84.0 137.8 %all-gather.13.cloned.1.call-start = ((), (), s32[]{:S(2)}) async-start(), calls=%async_computation.5 | async-start | bytes 4456448 | tf_op jit(solution)/shard_map/all_gather | solution.py:77
  84.9 170.7 %reduce-scatter.7.cloned.1.call-start = ((), (), s32[]{:S(2)}) async-start(), calls=%async_computation.9 | async-start | bytes 3342336
  131.1 161.2 %all-gather.11.cloned.1.call-start = ((), (), s32[]{:S(2)}) async-start(), calls=%async_computation.4 | async-start | bytes 1769472 | tf_op jit(solution)/shard_map/all_gather | solution.py:72
  131.3 9.8 %copy-start.7 = (s32[8192]{0:T(1024)S(1)}, s32[8192]{0:T(1024)}, u32[]{:S(2)}) copy-start(s32[8192]{0:T(1024)} %param.16) | copy-start | bytes 98308
  131.3 9.8 %copy-start.1 = (s32[12288]{0:T(1024)S(1)}, s32[12288]{0:T(1024)}, u32[]{:S(2)}) copy-start(s32[12288]{0:T(1024)} %param.13) | copy-start | bytes 147460
  141.1 193.1 %all-gather.17.cloned.1.call-start = ((), (), s32[]{:S(2)}) async-start(), calls=%async_computation.7 | async-start | bytes 1769472 | tf_op jit(solution)/shard_map/all_gather | solution.py:82
  226.5 149.9 %all-gather.15.cloned.1.call-start = ((), (), s32[]{:S(2)}) async-start(), calls=%async_computation.6 | async-start | bytes 1769472 | tf_op jit(solution)/shard_map/all_gather | solution.py:79
  231.3 297.5 %all-reduce.8.cloned.1.call-start = ((), (), s32[]{:S(2)}) async-start(), calls=%async_computation.11 | async-start | bytes 4194304 | tf_op jit(solution)/shard_map/psum | solution.py:98
  337.3 270.9 %reduce-scatter.9.cloned.1.call-start = ((), (), s32[]{:S(2)}) async-start(), calls=%async_computation.10 | async-start | bytes 3342336 | tf_op jit(solution)/shard_map/reduce_scatter | solution.py:84
  391.3 298.2 %all-reduce.10.cloned.1.call-start = ((), (), s32[]{:S(2)}) async-start(), calls=%async_computation.12 | async-start | bytes 4194304 | tf_op jit(solution)/shard_map/psum | solution.py:98
  528.8 317.5 %all-reduce.6.cloned.1.call-start = ((), (), s32[]{:S(2)}) async-start(), calls=%async_computation.8 | async-start | bytes 2097152 | tf_op jit(solution)/shard_map/psum | solution.py:109
  609.9 3.2 copy-start.5
  610.0 79.6 %copy-start.3 = (f32[512,512]{1,0:T(8,128)S(1)}, f32[512,512]{1,0:T(8,128)}, u32[]{:S(2)}) copy-start(f32[512,512]{1,0:T(8,128)} %param.15) | copy-start | bytes 3145732
  689.5 2.5 copy-start.4
  691.1 1.0 copy-start.2
Sparse Core Ops, SparseCore 0:
  11.1 67.6 all-gather.6
  84.1 31.9 all-gather.8
  119.1 60.9 all-gather.12
  184.0 71.5 reduce-scatter.6
  257.7 34.5 all-gather.10
  294.3 39.8 all-gather.16
  336.4 39.8 all-gather.14
  379.4 149.3 all-reduce.7
  532.9 75.3 reduce-scatter.8
  610.7 78.8 all-reduce.9
  694.9 151.3 all-reduce.5
